TPU v7x, 32 devices: a whole 2x2x4 slice. The times are simulated.
32 devices in a mesh: ctx: 4 (over z), row: 2 (over y), col: 4 (over x, core).
Axes of the slice: x: 2, y: 2, z: 4, core: 2. Of those that a mesh axis runs over, the one named last changes fastest.
Arguments:
- tokens: bfloat16 [2048, 8192], P(('ctx', 'row'), 'col'), may hold values from -9 to 9
- w_query: bfloat16 [8192, 2048], P('ctx', 'col'), may hold values from -0.0625 to 0.0625
- key_value_weight: bfloat16 [8192, 512], P('ctx', 'col'), may hold values from -0.0625 to 0.0625
- segment: int32 [2048], P(('ctx', 'row')), may hold values from 0 to 7, never falling along the last dimension, each value on 1 to 1024 neighbouring positions
Outputs:
- attended: bfloat16 [2048, 2048], P(('ctx', 'row'), 'col')
Inputs may be any that keep to these rules, and one draw needn't show every extreme that they name: `segment`: document ids never fall along the sequence; a document holds 1 to 1024 tokens.
All inputs are finite; a program needn't handle non-finite values.
Results may differ from a plain program's by a relative error of at most 0.011.
Values may be sent and summed in bfloat16 or wider, within the bound.
A program may use at most 64 MiB of HBM per device.

v0:
```python
import math

import jax
import jax.numpy as jnp
from jax import lax
from jax.sharding import PartitionSpec as P


def swapped(x, axis, stride):
    return lax.ppermute(x, axis, [(i, i ^ 1 << stride) for i in range(lax.axis_size(axis))])


def passed_along(x, axis, by):
    peers = lax.axis_size(axis)
    pairs = [(i, i + by) for i in range(peers) if 0 <= i + by < peers]
    return lax.ppermute(x, axis, pairs)


def local(tokens, w_query, key_value_weight, segment):
    half = tokens.shape[0]
    head_size = key_value_weight.shape[1]
    whole = lax.all_gather(tokens, "col", axis=1, tiled=True)
    query_acc = jnp.dot(
        whole,
        lax.all_gather(w_query, "ctx", axis=0, tiled=True),
        preferred_element_type=jnp.float32,
    )
    keyval_acc = jnp.dot(
        whole,
        lax.all_gather(key_value_weight, "ctx", axis=0, tiled=True),
        preferred_element_type=jnp.float32,
    )
    query = query_acc.astype(jnp.bfloat16)
    mine = keyval_acc.astype(jnp.bfloat16)
    is_even = lax.axis_index("col") % 2 == 0
    partner = swapped(mine, "col", 0)
    joined = jnp.concatenate(
        [jnp.where(is_even, mine, partner), jnp.where(is_even, partner, mine)], axis=1
    )
    block_kv, block_seg = (
        lax.all_gather(joined, "row", axis=0, tiled=True),
        lax.all_gather(segment, "row", axis=0, tiled=True),
    )
    prev_kv, prev_seg = passed_along((block_kv, block_seg), "ctx", 1)
    heads = query.shape[1] // head_size
    queries = query.reshape(half, heads, head_size)
    block = block_kv.shape[0]
    ctx_index = lax.axis_index("ctx")
    query_pos = lax.axis_index("row") * half + jnp.arange(half)
    key_pos = jnp.arange(block)
    own_allow = (key_pos[None, :] <= query_pos[:, None]) & (segment[:, None] == block_seg[None, :])
    prev_allow = (ctx_index > 0) & (segment[:, None] == prev_seg[None, :])
    scale = 1.0 / math.sqrt(head_size)

    def scores(key_value_rows, allow):
        score = (
            jnp.einsum(
                "qhd,kd->hqk",
                queries,
                key_value_rows[:, :head_size],
                preferred_element_type=jnp.float32,
            )
            * scale
        )
        return jnp.where(allow[None], score, -jnp.inf)

    parts = [(scores(block_kv, own_allow), block_kv), (scores(prev_kv, prev_allow), prev_kv)]
    top = parts[0][0].max(axis=-1, keepdims=True)
    for score, key_value_rows in parts[1:]:
        top = jnp.maximum(top, score.max(axis=-1, keepdims=True))
    total = jnp.zeros(top.shape[:2], jnp.float32)
    numer = jnp.zeros((half, heads, head_size), jnp.float32)
    for score, key_value_rows in parts:
        weight = jnp.exp(score - top)
        total = total + jnp.sum(weight, axis=-1)
        probs = weight.astype(jnp.bfloat16)
        numer = numer + jnp.einsum(
            "hqk,kd->qhd", probs, key_value_rows[:, head_size:], preferred_element_type=jnp.float32
        )
    result = (numer / jnp.transpose(total)[:, :, None]).astype(jnp.bfloat16)
    return result.reshape(half, heads * head_size)


def solution(mesh):
    in_specs = (P(("ctx", "row"), "col"), P("ctx", "col"), P("ctx", "col"), P(("ctx", "row")))
    out_specs = P(("ctx", "row"), "col")
    return jax.shard_map(local, mesh=mesh, in_specs=in_specs, out_specs=out_specs, check_vma=False)
```

profile of v0, /device:TPU:9, one launch (start us, length us, event | category | flops | bytes accessed | tf_op | source)
XLA Modules:
  0.0 262.2 jit_solution(787395383971608503)
XLA Ops:
  6.5 0.0 copy-start
  6.5 0.0 all-gather.7.cloned.1.call-start
  6.5 0.7 all-gather.7.cloned.1.call-update
  7.3 0.0 all-gather.5.cloned.1.call-start
  7.3 0.7 all-gather.5.cloned.1.call-update
  8.0 0.0 all-gather.9.cloned.1.call-start
  8.1 0.7 all-gather.9.cloned.1.call-update
  8.7 0.0 copy-done
  8.8 3.1 %all-gather = s32[2,1,256]{2,1,0:T(1,128)S(1)} all-gather(s32[1,1,256]{2,1,0:T(1,128)S(1)} %bitcast.56), channel_id=1, replica_groups=mesh['ctx'=4,'row'=2,'col'=4] {'row'}, dimensions={0}, use_global_device_ids=true | all-gather | bytes 3072 | tf_op jit(solution)/shard_map/all_gather | solution.py:42
  11.8 3.2 %collective-permute-start.1 = (s32[512]{0:T(512)S(1)}, s32[512]{0:T(512)S(1)}, u32[]{:S(2)}, u32[]{:S(2)}) collective-permute-start(s32[512]{0:T(512)S(1)} %bitcast.54), channel_id=1, source_target_pairs={{0,8},{8,16},{16,24},{1,9},{9,17},{17,25},{2,10},{10,18},{18,26},{... | collective-permute-start | bytes 6152 | tf_op jit(solution)/shard_map/ppermute | solution.py:16
  15.1 39.1 %all-gather.7.cloned.1.call-done = bf16[8192,128]{1,0:T(8,128)(2,1)} async-done(((bf16[2048,128]{1,0:T(8,128)(2,1)}), bf16[8192,128]{1,0:T(8,128)(2,1)}) %all-gather.7.cloned.1.call-update) | async-done | bytes 2097168 | tf_op jit(solution)/shard_map/all_gather | solution.py:30
  54.2 37.1 %all-gather.5.cloned.1.call-done = bf16[256,8192]{1,0:T(8,128)(2,1)} async-done(((bf16[256,2048]{1,0:T(8,128)(2,1)}), bf16[256,8192]{1,0:T(8,128)(2,1)}) %all-gather.5.cloned.1.call-update) | async-done | bytes 4194320 | tf_op jit(solution)/shard_map/all_gather | solution.py:22
  91.3 4.4 %convolution_convert_fusion.1 = bf16[256,128]{0,1:T(8,128)(2,1)S(1)} fusion(bf16[256,8192]{1,0:T(8,128)(2,1)} %all-gather.5.cloned.1.call-done, bf16[8192,128]{1,0:T(8,128)(2,1)} %all-gather.7.cloned.1.call-done), kind=kOutput, calls=%fused_computation.15 | convolution fusion | flops 536903680 | bytes 6356992 | tf_op jit(solution)/shard_map/dot_general | solution.py:28
  95.7 0.3 collective-permute-start
  96.0 0.0 collective-permute-done.1
  96.0 0.3 compare_and_fusion
  96.2 0.7 collective-permute-done
  97.0 5.5 %all_gather.17 = bf16[512,256]{0,1:T(8,128)(2,1)S(1)} all-gather(bf16[256,256]{0,1:T(8,128)(2,1)S(1)} %pad_maximum_fusion), channel_id=1, replica_groups=mesh['ctx'=4,'row'=2,'col'=4] {'row'}, dimensions={0}, use_global_device_ids=true | all-gather | bytes 393216 | tf_op jit(solution)/shard_map/all_gather | solution.py:41
  102.5 3.1 %collective-permute-start.2 = (bf16[512,256]{0,1:T(8,128)(2,1)S(1)}, bf16[512,256]{0,1:T(8,128)(2,1)S(1)}, u32[]{:S(2)}, u32[]{:S(2)}) collective-permute-start(bf16[512,256]{0,1:T(8,128)(2,1)S(1)} %all_gather.17), channel_id=1, source_target_pairs={{0,8},{8,16},{16,24},{1,9},{9,17},{17,25},{2,10},{10,18},{18,26},{... | collective-permute-start | bytes 786440 | tf_op jit(solution)/shard_map/ppermute | solution.py:16
  105.6 139.3 %all-gather.9.cloned.1.call-done = bf16[8192,512]{1,0:T(8,128)(2,1)} async-done(((bf16[2048,512]{1,0:T(8,128)(2,1)}), bf16[8192,512]{1,0:T(8,128)(2,1)}) %all-gather.9.cloned.1.call-update) | async-done | bytes 8388624 | tf_op jit(solution)/shard_map/all_gather | solution.py:25
  244.9 7.0 %fusion.8 = bf16[32,4,8,128]{3,2,1,0:T(8,128)(2,1)S(1)} fusion(bf16[256,8192]{1,0:T(8,128)(2,1)} %all-gather.5.cloned.1.call-done, bf16[8192,512]{1,0:T(8,128)(2,1)} %all-gather.9.cloned.1.call-done), kind=kOutput, calls=%fused_computation.14 | convolution fusion | flops 2147614720 | bytes 12845056 | tf_op jit(solution)/shard_map/dot_general | solution.py:23
  251.9 0.5 fusion.25
  252.4 0.0 collective-permute-done.2
  252.4 0.5 fusion.4
  252.9 0.5 fusion.10
  253.4 0.7 fusion.2
  254.2 0.7 fusion.7
  254.9 0.8 copy.18
  (5 shorter events, 0.0 us)
Async XLA Ops:
  6.5 2.2 copy-start
  6.5 47.7 %all-gather.7.cloned.1.call-start = ((), (), s32[]{:S(2)}) async-start(), calls=%async_computation.1 | async-start | bytes 2621440 | tf_op jit(solution)/shard_map/all_gather | solution.py:30
  7.3 84.0 %all-gather.5.cloned.1.call-start = ((), (), s32[]{:S(2)}) async-start(), calls=%async_computation | async-start | bytes 5242880 | tf_op jit(solution)/shard_map/all_gather | solution.py:22
  8.0 236.9 %all-gather.9.cloned.1.call-start = ((), (), s32[]{:S(2)}) async-start(), calls=%async_computation.2 | async-start | bytes 10485760 | tf_op jit(solution)/shard_map/all_gather | solution.py:25
  11.8 84.1 %collective-permute-start.1 = (s32[512]{0:T(512)S(1)}, s32[512]{0:T(512)S(1)}, u32[]{:S(2)}, u32[]{:S(2)}) collective-permute-start(s32[512]{0:T(512)S(1)} %bitcast.54), channel_id=1, source_target_pairs={{0,8},{8,16},{16,24},{1,9},{9,17},{17,25},{2,10},{10,18},{18,26},{... | collective-permute-start | bytes 6152 | tf_op jit(solution)/shard_map/ppermute | solution.py:16
  95.7 1.3 collective-permute-start
  102.5 149.9 %collective-permute-start.2 = (bf16[512,256]{0,1:T(8,128)(2,1)S(1)}, bf16[512,256]{0,1:T(8,128)(2,1)S(1)}, u32[]{:S(2)}, u32[]{:S(2)}) collective-permute-start(bf16[512,256]{0,1:T(8,128)(2,1)S(1)} %all_gather.17), channel_id=1, source_target_pairs={{0,8},{8,16},{16,24},{1,9},{9,17},{17,25},{2,10},{10,18},{18,26},{... | collective-permute-start | bytes 786440 | tf_op jit(solution)/shard_map/ppermute | solution.py:16
Sparse Core Ops, SparseCore 0:
  8.9 45.2 all-gather.6
  55.8 35.4 all-gather.4
  92.8 152.0 all-gather.8
where the time goes:
time: 263 us; the launch traced here: 262 us
  waiting for transfers between devices  218 us (83%)
  matrix products  13.5 us (5%)
  between operations  13.2 us (5%)
  blocking collectives  8.61 us (3%)
  starting transfers between devices  6.7 us (3%)
    all_gather x1, waiting for transfers between devices, local(): lax.all_gather(w_query, 'ctx', axis=0, tiled=True)  139 us
    all_gather x1, waiting for transfers between devices, local(): lax.all_gather(key_value_weight, 'ctx', axis=0, tiled=True)  39.1 us
    all_gather x1, waiting for transfers between devices, local(): whole = lax.all_gather(tokens, 'col', axis=1, tiled=True)  37.1 us
    dot_general x1, matrix products, local(): jnp.dot(whole, lax.all_gather(w_query, 'ctx', axis=0, tiled=True), prefer...  6.98 us
    ppermute x2, starting transfers between devices, passed_along(): return lax.ppermute(x, axis, pairs)  6.29 us
    all_gather x1, blocking collectives, local(): lax.all_gather(joined, 'row', axis=0, tiled=True)  5.51 us
  transfers between devices with their start and end apart: 6, of which 4 were waited for; matrix products, arithmetic and copies ran while one was open for 5% of the time, Pallas kernels for 0%

commit v1 on v0

v1 whole, which is shorter than its diff:
```python
import functools
import math

import jax
import jax.numpy as jnp
from jax import lax
from jax.experimental import pallas as pl
from jax.experimental.pallas import tpu as pltpu
from jax.sharding import PartitionSpec as P

MESH = pl.DeviceIdType.MESH


def kernel(
    n, head, tok_hbm, wq_hbm, wkv_hbm, seg_ref, out_ref,
    whole, weights, part, landed, own, query, window, segs,
    w_sem, a2a_send, tok_recv, fwd_send, part_send, part_recv, kv_send, kv_recv, seg_send, seg_recv,
):
    c, r, k = lax.axis_index("ctx"), lax.axis_index("row"), lax.axis_index("col")
    half = tok_hbm.shape[0]
    rows = half // n
    width = weights.shape[1]
    even = k % 2 == 0

    w_copies = [
        pltpu.make_async_copy(wkv_hbm, weights.at[:, pl.ds(0, head)], w_sem.at[0]),
        pltpu.make_async_copy(wq_hbm, weights.at[:, pl.ds(head, width - head)], w_sem.at[1]),
    ]
    for copy in w_copies:
        copy.start()

    barrier = pltpu.get_barrier_semaphore()

    def greet(i, carry):
        c2, k2 = i // n, i % n

        @pl.when(i != c * n + k)
        def _():
            pl.semaphore_signal(barrier, inc=1, device_id=(c2, r, k2), device_id_type=MESH)

        return carry

    lax.fori_loop(0, n * n, greet, 0)
    for dc in (-1, 0, 1):

        @pl.when((c + dc >= 0) & (c + dc < n))
        def _():
            for dk in (0, 1):
                pl.semaphore_signal(barrier, inc=1, device_id=(c + dc, 1 - r, k ^ dk), device_id_type=MESH)

    ends = jnp.where(c == 0, 1, 0) + jnp.where(c == n - 1, 1, 0)
    pl.semaphore_wait(barrier, n * n - 1 + 6 - 2 * ends)

    def piece(block, j):
        return whole.at[block, pl.ds(pl.multiple_of(j * rows, rows), rows)]

    def landing(ref, sem):
        return pltpu.make_async_copy(ref, ref, sem)

    order = [m for m in range(n) if m & 2] + [m for m in range(n) if not m & 2]

    def scatter(m):
        j = k ^ m
        return pltpu.make_async_remote_copy(
            src_ref=tok_hbm.at[pl.ds(pl.multiple_of(j * rows, rows), rows)],
            dst_ref=piece(c, j),
            send_sem=a2a_send.at[m],
            recv_sem=tok_recv.at[c, j],
            device_id=(k, r, j),
            device_id_type=MESH,
        )

    for m in order:
        if m == 0:

            @pl.when(c == k)
            def _():
                pltpu.make_async_copy(
                    tok_hbm.at[pl.ds(pl.multiple_of(k * rows, rows), rows)], piece(c, k), tok_recv.at[c, k]
                ).start()

            @pl.when(c != k)
            def _():
                scatter(0).start()

        else:
            scatter(m).start()

    seg_slot = 2 + r

    def seg_copy(i):
        dc, r2 = ((0, 1 - r), (1, r), (1, 1 - r))[i]
        slot = 2 + r if dc == 0 else r
        return pltpu.make_async_remote_copy(
            src_ref=seg_ref, dst_ref=segs.at[slot], send_sem=seg_send.at[i], recv_sem=seg_recv.at[slot],
            device_id=(c + dc, r2, k), device_id_type=MESH,
        )

    seg_copy(0).start()

    @pl.when(c < n - 1)
    def _():
        seg_copy(1).start()
        seg_copy(2).start()

    segs[seg_slot] = seg_ref[...]

    def forward(s, block, j, to, index):
        return pltpu.make_async_remote_copy(
            src_ref=piece(block, j), dst_ref=piece(block, j),
            send_sem=fwd_send.at[s, index], recv_sem=tok_recv.at[block, j],
            device_id=(c, r, to), device_id_type=MESH,
        )

    peers = list(range(2, n, 2))

    def step_a(s):
        block = c ^ s
        landing(piece(block, k), tok_recv.at[block, k]).wait()
        for i, m in enumerate(peers):
            forward(s, block, k, k ^ m, i).start()
        forward(s, block, k, k ^ 1, len(peers)).start()

    def step_b(s):
        block = c ^ s
        for i, m in enumerate(peers):
            landing(piece(block, k ^ m), tok_recv.at[block, k ^ m]).wait()
            forward(s, block, k ^ m, k ^ 1, len(peers) + 1 + i).start()

    def part_copy(s):
        return pltpu.make_async_remote_copy(
            src_ref=part.at[s - 1], dst_ref=landed.at[s - 1],
            send_sem=part_send.at[s - 1], recv_sem=part_recv.at[s - 1],
            device_id=(c ^ s, r, k), device_id_type=MESH,
        )

    spans = [(0, head)] + [(lo, min(256, width - lo)) for lo in range(head, width, 256)]

    def step_c(s):
        block = c ^ s
        for m in [0] + peers:
            landing(piece(block, k ^ 1 ^ m), tok_recv.at[block, k ^ 1 ^ m]).wait()
        if s == 0:
            for copy in w_copies:
                copy.wait()
        for lo, size in spans:
            product = jnp.dot(whole[block], weights[:, lo : lo + size], preferred_element_type=jnp.float32)
            if s == 0:
                own[:, lo : lo + size] = product
            else:
                part[s - 1, :, lo : lo + size] = product.astype(jnp.bfloat16)
        if s:
            part_copy(s).start()

    for t in range(n + 2):
        if t < n:
            step_a(t)
        if 0 <= t - 1 < n:
            step_b(t - 1)
        if 0 <= t - 2 < n:
            step_c(t - 2)

    for s in range(1, n):
        landing(landed.at[s - 1], part_recv.at[s - 1]).wait()

    def summed(lo, size):
        total = own[:, lo : lo + size]
        for s in range(1, n):
            total = total + landed[s - 1, :, lo : lo + size].astype(jnp.float32)
        return total.astype(jnp.bfloat16)

    kind = k % 2
    window[kind, 2 + r] = summed(0, head)

    def kv_copy(i):
        dc, dr, dk = i // 4, (i // 2) % 2, i % 2
        r2 = 1 - r if dr else r
        slot = 2 + r if dc == 0 else r
        return pltpu.make_async_remote_copy(
            src_ref=window.at[kind, 2 + r], dst_ref=window.at[kind, slot],
            send_sem=kv_send.at[i], recv_sem=kv_recv.at[kind, slot],
            device_id=(c + dc, r2, k ^ dk), device_id_type=MESH,
        )

    @pl.when(c < n - 1)
    def _():
        for i in (6, 7, 4, 5):
            kv_copy(i).start()

    for i in (2, 3, 1):
        kv_copy(i).start()

    @pl.when(c == 0)
    def _():
        for slot in (0, 1):
            for which in (0, 1):
                window[which, slot] = jnp.zeros((half, head), jnp.bfloat16)
            segs[slot] = jnp.zeros(segs.shape[1:], jnp.int32)

    query[...] = summed(head, width - head)

    landing(segs.at[3 - r], seg_recv.at[3 - r]).wait()

    @pl.when(c > 0)
    def _():
        for slot in (0, 1):
            landing(segs.at[slot], seg_recv.at[slot]).wait()

    key_seg = jnp.concatenate([segs[i][:1] for i in range(4)], axis=1)
    mine = jnp.transpose(jnp.broadcast_to(seg_ref[:1], (128, half)))[:, :1]
    keys_n = 4 * half
    key_pos = lax.broadcasted_iota(jnp.int32, (half, keys_n), 1)
    query_pos = lax.broadcasted_iota(jnp.int32, (half, keys_n), 0) + (2 + r) * half
    first = jnp.where(c == 0, 2 * half, 0)
    allow = (key_pos <= query_pos) & (mine == key_seg) & (key_pos >= first)

    landing(window.at[1 - kind, 2 + r], kv_recv.at[1 - kind, 2 + r]).wait()
    for which in (0, 1):
        landing(window.at[which, 3 - r], kv_recv.at[which, 3 - r]).wait()

    @pl.when(c > 0)
    def _():
        for which in (0, 1):
            for slot in (0, 1):
                landing(window.at[which, slot], kv_recv.at[which, slot]).wait()

    keys = window[0].reshape(keys_n, head)
    values = window[1].reshape(keys_n, head)
    scale = 1.0 / math.sqrt(head)
    for h in range((width - head) // head):
        score = lax.dot_general(
            query[:, h * head : (h + 1) * head], keys, (((1,), (1,)), ((), ())), preferred_element_type=jnp.float32
        )
        score = jnp.where(allow, score * scale, -jnp.inf)
        weight = jnp.exp(score - jnp.max(score, axis=1, keepdims=True))
        total = jnp.sum(weight, axis=1, keepdims=True)
        numer = jnp.dot(weight.astype(jnp.bfloat16), values, preferred_element_type=jnp.float32)
        out_ref[:, h * head : (h + 1) * head] = (numer / total).astype(jnp.bfloat16)

    for m in range(1, n):
        scatter(m).wait_send()

    @pl.when(c != k)
    def _():
        scatter(0).wait_send()

    for s in range(n):
        block = c ^ s
        for i in range(2 * len(peers) + 1):
            forward(s, block, k, k ^ 1, i).wait_send()
    for s in range(1, n):
        part_copy(s).wait_send()
    for i in (1, 2, 3):
        kv_copy(i).wait_send()
    seg_copy(0).wait_send()

    @pl.when(c < n - 1)
    def _():
        for i in (4, 5, 6, 7):
            kv_copy(i).wait_send()
        seg_copy(1).wait_send()
        seg_copy(2).wait_send()


def local(n, tokens, w_query, key_value_weight, segment):
    half, depth = tokens.shape
    head = key_value_weight.shape[1]
    width = head + w_query.shape[1]
    seg = jnp.broadcast_to(segment[None, :], (8, half))
    hbm = pl.BlockSpec(memory_space=pl.ANY)
    vmem = pl.BlockSpec(memory_space=pltpu.VMEM)
    dma = pltpu.SemaphoreType.DMA
    return pl.pallas_call(
        functools.partial(kernel, n, head),
        out_shape=jax.ShapeDtypeStruct((half, w_query.shape[1]), jnp.bfloat16),
        in_specs=[hbm, hbm, hbm, vmem],
        out_specs=vmem,
        scratch_shapes=[
            pltpu.VMEM((n, half, depth), jnp.bfloat16),
            pltpu.VMEM((depth, width), jnp.bfloat16),
            pltpu.VMEM((n - 1, half, width), jnp.bfloat16),
            pltpu.VMEM((n - 1, half, width), jnp.bfloat16),
            pltpu.VMEM((half, width), jnp.float32),
            pltpu.VMEM((half, width - head), jnp.bfloat16),
            pltpu.VMEM((2, 4, half, head), jnp.bfloat16),
            pltpu.VMEM((4, 8, half), jnp.int32),
            dma((2,)),
            dma((n,)),
            dma((n, n)),
            dma((n, n)),
            dma((n - 1,)),
            dma((n - 1,)),
            dma((8,)),
            dma((2, 4)),
            dma((3,)),
            dma((4,)),
        ],
        compiler_params=pltpu.CompilerParams(
            collective_id=0, has_side_effects=True, vmem_limit_bytes=50 * 2**20
        ),
    )(tokens, w_query, key_value_weight, seg)


def solution(mesh):
    in_specs = (P(("ctx", "row"), "col"), P("ctx", "col"), P("ctx", "col"), P(("ctx", "row")))
    out_specs = P(("ctx", "row"), "col")
    step = functools.partial(local, mesh.shape["ctx"])
    return jax.shard_map(step, mesh=mesh, in_specs=in_specs, out_specs=out_specs, check_vma=False)
```

time: 263 us -> 97.9 us (0.37)
  the two profiles are of different devices: /device:TPU:9 before, /device:TPU:17 now
where the time goes in v1:
time: 97.9 us; the launch traced here: 97.7 us
  Pallas kernels  92.4 us (94%)
  local copies, waits for them, and re-layouts  5.24 us (5%)
    pallas_call x1, Pallas kernels, local(): pl.pallas_call(functools.partial(kernel, n, head), out_shape=jax.ShapeDty...  92.4 us
    unnamed x7, local copies, waits for them, and re-layouts  4.56 us

profile of v1, /device:TPU:17, one launch (start us, length us, event | category | flops | bytes accessed | tf_op | source)
XLA Modules:
  0.0 97.7 jit_solution(13577676462013656902)
XLA Ops:
  0.0 0.7 broadcast_in_dim.2.seg_ref
  0.7 0.0 copy-start
  0.7 1.6 %copy-done = bf16[2048,512]{1,0:T(8,128)(2,1)S(1)} copy-done((bf16[2048,512]{1,0:T(8,128)(2,1)S(1)}, bf16[2048,512]{1,0:T(8,128)(2,1)}, u32[]{:S(2)}) %copy-start) | copy-done | bytes 2097176
  2.3 0.0 copy-start.1
  2.3 1.2 %copy-done.1 = bf16[256,2048]{1,0:T(8,128)(2,1)S(1)} copy-done((bf16[256,2048]{1,0:T(8,128)(2,1)S(1)}, bf16[256,2048]{1,0:T(8,128)(2,1)}, u32[]{:S(2)}) %copy-start.1) | copy-done | bytes 1048600
  3.5 0.0 copy-start.2
  3.5 1.0 %copy-done.2 = bf16[2048,128]{1,0:T(8,128)(2,1)S(1)} copy-done((bf16[2048,128]{1,0:T(8,128)(2,1)S(1)}, bf16[2048,128]{1,0:T(8,128)(2,1)}, u32[]{:S(2)}) %copy-start.2) | copy-done | bytes 524312
  4.5 92.4 %shard_map.46 = bf16[256,512]{1,0:T(8,128)(2,1)S(1)} custom-call(bf16[256,2048]{1,0:T(8,128)(2,1)S(1)} %copy-done.1, bf16[2048,512]{1,0:T(8,128)(2,1)S(1)} %copy-done, bf16[2048,128]{1,0:T(8,128)(2,1)S(1)} %copy-done.2, s32[8,256]{1,0:T(8,128)S(1)} %broadcast_in_dim.2.seg_ref), custom_call_target="tpu_custom_call" | custom-call | tf_op jit(solution)/shard_map/pallas_call | solution.py:273
  97.0 0.7 copy.6
Async XLA Ops:
  0.7 1.6 %copy-start = (bf16[2048,512]{1,0:T(8,128)(2,1)S(1)}, bf16[2048,512]{1,0:T(8,128)(2,1)}, u32[]{:S(2)}) copy-start(bf16[2048,512]{1,0:T(8,128)(2,1)} %wq_hbm.1) | copy-start | bytes 6291460
  2.3 1.2 %copy-start.1 = (bf16[256,2048]{1,0:T(8,128)(2,1)S(1)}, bf16[256,2048]{1,0:T(8,128)(2,1)}, u32[]{:S(2)}) copy-start(bf16[256,2048]{1,0:T(8,128)(2,1)} %tok_hbm.1) | copy-start | bytes 3145732
  3.5 1.0 %copy-start.2 = (bf16[2048,128]{1,0:T(8,128)(2,1)S(1)}, bf16[2048,128]{1,0:T(8,128)(2,1)}, u32[]{:S(2)}) copy-start(bf16[2048,128]{1,0:T(8,128)(2,1)} %wkv_hbm.1) | copy-start | bytes 1572868

commit v2 on v1

--- a/solution.py
+++ b/solution.py
@@ -13,8 +13,8 @@
 
 def kernel(
     n, head, tok_hbm, wq_hbm, wkv_hbm, seg_ref, out_ref,
-    whole, weights, part, landed, own, query, window, segs,
-    w_sem, a2a_send, tok_recv, fwd_send, part_send, part_recv, kv_send, kv_recv, seg_send, seg_recv,
+    whole, staged, weights, part, landed, own, query, window, segs,
+    w_sem, a2a_send, stage_recv, relay_send, tok_recv, fwd_send, part_send, part_recv, kv_send, kv_recv, seg_send, seg_recv,
 ):
     c, r, k = lax.axis_index("ctx"), lax.axis_index("row"), lax.axis_index("col")
     half = tok_hbm.shape[0]
@@ -57,42 +57,54 @@
     def landing(ref, sem):
         return pltpu.make_async_copy(ref, ref, sem)
 
-    order = [m for m in range(n) if m & 2] + [m for m in range(n) if not m & 2]
-
-    def scatter(m):
+    own_plane = c == k
+
+    def token_rows(j):
+        return tok_hbm.at[pl.ds(pl.multiple_of(j * rows, rows), rows)]
+
+    def scatter(m, plane):
         j = k ^ m
         return pltpu.make_async_remote_copy(
-            src_ref=tok_hbm.at[pl.ds(pl.multiple_of(j * rows, rows), rows)],
-            dst_ref=piece(c, j),
-            send_sem=a2a_send.at[m],
-            recv_sem=tok_recv.at[c, j],
-            device_id=(k, r, j),
-            device_id_type=MESH,
-        )
-
-    for m in order:
-        if m == 0:
-
-            @pl.when(c == k)
-            def _():
-                pltpu.make_async_copy(
-                    tok_hbm.at[pl.ds(pl.multiple_of(k * rows, rows), rows)], piece(c, k), tok_recv.at[c, k]
-                ).start()
-
-            @pl.when(c != k)
-            def _():
-                scatter(0).start()
-
-        else:
-            scatter(m).start()
-
-    seg_slot = 2 + r
+            src_ref=token_rows(j), dst_ref=piece(c, j), send_sem=a2a_send.at[m], recv_sem=tok_recv.at[c, j],
+            device_id=(plane, r, j), device_id_type=MESH,
+        )
+
+    def stage(m):
+        j = k ^ m
+        return pltpu.make_async_remote_copy(
+            src_ref=token_rows(j), dst_ref=staged.at[m], send_sem=a2a_send.at[m], recv_sem=stage_recv.at[m],
+            device_id=(c, r, j), device_id_type=MESH,
+        )
+
+    def relay(m):
+        return pltpu.make_async_remote_copy(
+            src_ref=staged.at[m], dst_ref=piece(c, k), send_sem=relay_send.at[m], recv_sem=tok_recv.at[c, k],
+            device_id=(k ^ m, r, k), device_id_type=MESH,
+        )
+
+    far = list(range(2, n))
+
+    @pl.when(own_plane)
+    def _():
+        for m in far:
+            scatter(m, c).start()
+        pltpu.make_async_copy(token_rows(k), piece(c, k), tok_recv.at[c, k]).start()
+        scatter(1, c).start()
+
+    @pl.when(c != k)
+    def _():
+        for m in far:
+            stage(m).start()
+        for m in (1, 0):
+            scatter(m, k).start()
+
+    segs[2 + r] = jnp.broadcast_to(seg_ref[...], segs.shape[1:])
 
     def seg_copy(i):
         dc, r2 = ((0, 1 - r), (1, r), (1, 1 - r))[i]
         slot = 2 + r if dc == 0 else r
         return pltpu.make_async_remote_copy(
-            src_ref=seg_ref, dst_ref=segs.at[slot], send_sem=seg_send.at[i], recv_sem=seg_recv.at[slot],
+            src_ref=segs.at[2 + r], dst_ref=segs.at[slot], send_sem=seg_send.at[i], recv_sem=seg_recv.at[slot],
             device_id=(c + dc, r2, k), device_id_type=MESH,
         )
 
@@ -103,7 +115,12 @@
         seg_copy(1).start()
         seg_copy(2).start()
 
-    segs[seg_slot] = seg_ref[...]
+    for m in far:
+
+        @pl.when(c != k ^ m)
+        def _():
+            landing(staged.at[m], stage_recv.at[m]).wait()
+            relay(m).start()
 
     def forward(s, block, j, to, index):
         return pltpu.make_async_remote_copy(
@@ -207,7 +224,7 @@
             landing(segs.at[slot], seg_recv.at[slot]).wait()
 
     key_seg = jnp.concatenate([segs[i][:1] for i in range(4)], axis=1)
-    mine = jnp.transpose(jnp.broadcast_to(seg_ref[:1], (128, half)))[:, :1]
+    mine = jnp.transpose(jnp.broadcast_to(seg_ref[...], (128, half)))[:, :1]
     keys_n = 4 * half
     key_pos = lax.broadcasted_iota(jnp.int32, (half, keys_n), 1)
     query_pos = lax.broadcasted_iota(jnp.int32, (half, keys_n), 0) + (2 + r) * half
@@ -238,11 +255,17 @@
         out_ref[:, h * head : (h + 1) * head] = (numer / total).astype(jnp.bfloat16)
 
     for m in range(1, n):
-        scatter(m).wait_send()
+        stage(m).wait_send()
 
     @pl.when(c != k)
     def _():
-        scatter(0).wait_send()
+        stage(0).wait_send()
+
+    for m in far:
+
+        @pl.when(c != k ^ m)
+        def _():
+            relay(m).wait_send()
 
     for s in range(n):
         block = c ^ s
@@ -266,7 +289,6 @@
     half, depth = tokens.shape
     head = key_value_weight.shape[1]
     width = head + w_query.shape[1]
-    seg = jnp.broadcast_to(segment[None, :], (8, half))
     hbm = pl.BlockSpec(memory_space=pl.ANY)
     vmem = pl.BlockSpec(memory_space=pltpu.VMEM)
     dma = pltpu.SemaphoreType.DMA
@@ -277,6 +299,7 @@
         out_specs=vmem,
         scratch_shapes=[
             pltpu.VMEM((n, half, depth), jnp.bfloat16),
+            pltpu.VMEM((n, half // n, depth), jnp.bfloat16),
             pltpu.VMEM((depth, width), jnp.bfloat16),
             pltpu.VMEM((n - 1, half, width), jnp.bfloat16),
             pltpu.VMEM((n - 1, half, width), jnp.bfloat16),
@@ -285,6 +308,8 @@
             pltpu.VMEM((2, 4, half, head), jnp.bfloat16),
             pltpu.VMEM((4, 8, half), jnp.int32),
             dma((2,)),
+            dma((n,)),
+            dma((n,)),
             dma((n,)),
             dma((n, n)),
             dma((n, n)),
@@ -296,9 +321,9 @@
             dma((4,)),
         ],
         compiler_params=pltpu.CompilerParams(
-            collective_id=0, has_side_effects=True, vmem_limit_bytes=50 * 2**20
+            collective_id=0, has_side_effects=True, vmem_limit_bytes=60 * 2**20
         ),
-    )(tokens, w_query, key_value_weight, seg)
+    )(tokens, w_query, key_value_weight, segment[None, :])
 
 
 def solution(mesh):

time: 97.9 us -> 84.7 us (0.87)
  the two profiles are of different devices: /device:TPU:17 before, /device:TPU:19 now
where the time goes in v2:
time: 84.7 us; the launch traced here: 84.6 us
  Pallas kernels  82.9 us (98%)
  local copies, waits for them, and re-layouts  1.67 us (2%)
    pallas_call x1, Pallas kernels, local(): pl.pallas_call(functools.partial(kernel, n, head), out_shape=jax.ShapeDty...  82.9 us

profile of v2, /device:TPU:19, one launch (start us, length us, event | category | flops | bytes accessed | tf_op | source)
XLA Modules:
  0.0 84.6 jit_solution(12649573142628229858)
XLA Ops:
  0.0 82.9 %shard_map.46 = bf16[256,512]{1,0:T(8,128)(2,1)} custom-call(bf16[256,2048]{1,0:T(8,128)(2,1)} %tok_hbm.1, bf16[2048,512]{1,0:T(8,128)(2,1)} %wq_hbm.1, bf16[2048,128]{1,0:T(8,128)(2,1)} %wkv_hbm.1, s32[1,256]{1,0:T(1,128)} %bitcast.1), custom_call_target="tpu_custom_call" | custom-call | tf_op jit(solution)/shard_map/pallas_call | solution.py:295
  82.9 1.7 %copy.6 = bf16[256,512]{1,0:T(8,128)(2,1)} copy(bf16[256,512]{1,0:T(8,128)(2,1)} %shard_map.46) | data formatting | bytes 524288

commit v3 on v2

--- a/solution.py
+++ b/solution.py
@@ -13,14 +13,20 @@
 
 def kernel(
     n, head, tok_hbm, wq_hbm, wkv_hbm, seg_ref, out_ref,
-    whole, staged, weights, part, landed, own, query, window, segs,
-    w_sem, a2a_send, stage_recv, relay_send, tok_recv, fwd_send, part_send, part_recv, kv_send, kv_recv, seg_send, seg_recv,
+    whole, staged, weights, part, landed, transit, far_own, own, query, window, segs,
+    w_sem, a2a_send, stage_recv, relay_send, tok_recv, fwd_send, part_send, part_recv, transit_recv, kv_send, kv_recv, seg_send, seg_recv,
 ):
     c, r, k = lax.axis_index("ctx"), lax.axis_index("row"), lax.axis_index("col")
     half = tok_hbm.shape[0]
     rows = half // n
     width = weights.shape[1]
-    even = k % 2 == 0
+    paired = n == 4
+    inner = (c == 1) | (c == 2)
+
+    def block_of(s):
+        if paired and s >= 2:
+            return jnp.where(c < 2, s, 3 - s)
+        return c ^ s
 
     w_copies = [
         pltpu.make_async_copy(wkv_hbm, weights.at[:, pl.ds(0, head)], w_sem.at[0]),
@@ -132,29 +138,41 @@
     peers = list(range(2, n, 2))
 
     def step_a(s):
-        block = c ^ s
+        block = block_of(s)
         landing(piece(block, k), tok_recv.at[block, k]).wait()
         for i, m in enumerate(peers):
             forward(s, block, k, k ^ m, i).start()
         forward(s, block, k, k ^ 1, len(peers)).start()
 
     def step_b(s):
-        block = c ^ s
+        block = block_of(s)
         for i, m in enumerate(peers):
             landing(piece(block, k ^ m), tok_recv.at[block, k ^ m]).wait()
             forward(s, block, k ^ m, k ^ 1, len(peers) + 1 + i).start()
 
-    def part_copy(s):
-        return pltpu.make_async_remote_copy(
-            src_ref=part.at[s - 1], dst_ref=landed.at[s - 1],
-            send_sem=part_send.at[s - 1], recv_sem=part_recv.at[s - 1],
-            device_id=(c ^ s, r, k), device_id_type=MESH,
+    chunk = half // 2
+
+    def part_copy(s, i):
+        lines = pl.ds(i * chunk, chunk)
+        slot = 1 if paired and s >= 2 else s - 1
+        return pltpu.make_async_remote_copy(
+            src_ref=part.at[s - 1, lines], dst_ref=landed.at[slot, lines],
+            send_sem=part_send.at[s - 1, i], recv_sem=part_recv.at[slot, i],
+            device_id=(block_of(s), r, k), device_id_type=MESH,
+        )
+
+    def hand_over(s, i):
+        lines = pl.ds(i * chunk, chunk)
+        return pltpu.make_async_remote_copy(
+            src_ref=part.at[s - 1, lines], dst_ref=transit.at[s - 2, lines],
+            send_sem=part_send.at[s - 1, i], recv_sem=transit_recv.at[s - 2, i],
+            device_id=(c ^ 1, r, k), device_id_type=MESH,
         )
 
     spans = [(0, head)] + [(lo, min(256, width - lo)) for lo in range(head, width, 256)]
 
     def step_c(s):
-        block = c ^ s
+        block = block_of(s)
         for m in [0] + peers:
             landing(piece(block, k ^ 1 ^ m), tok_recv.at[block, k ^ 1 ^ m]).wait()
         if s == 0:
@@ -166,8 +184,28 @@
                 own[:, lo : lo + size] = product
             else:
                 part[s - 1, :, lo : lo + size] = product.astype(jnp.bfloat16)
-        if s:
-            part_copy(s).start()
+                if paired and s >= 2:
+                    far_own[s - 2, :, lo : lo + size] = product
+        if paired and s >= 2:
+
+            @pl.when(jnp.logical_not(inner))
+            def _():
+                for i in (0, 1):
+                    hand_over(s, i).start()
+
+        elif s:
+            for i in (0, 1):
+                part_copy(s, i).start()
+
+    def combine(s):
+        @pl.when(inner)
+        def _():
+            for i in (0, 1):
+                lines = pl.ds(i * chunk, chunk)
+                landing(transit.at[s - 2, lines], transit_recv.at[s - 2, i]).wait()
+                total = far_own[s - 2, lines] + transit[s - 2, lines].astype(jnp.float32)
+                part[s - 1, lines] = total.astype(jnp.bfloat16)
+                part_copy(s, i).start()
 
     for t in range(n + 2):
         if t < n:
@@ -177,13 +215,19 @@
         if 0 <= t - 2 < n:
             step_c(t - 2)
 
-    for s in range(1, n):
-        landing(landed.at[s - 1], part_recv.at[s - 1]).wait()
+    if paired:
+        combine(2)
+        combine(3)
+
+    slots = landed.shape[0]
+    for slot in range(slots):
+        for i in (0, 1):
+            landing(landed.at[slot, pl.ds(i * chunk, chunk)], part_recv.at[slot, i]).wait()
 
     def summed(lo, size):
         total = own[:, lo : lo + size]
-        for s in range(1, n):
-            total = total + landed[s - 1, :, lo : lo + size].astype(jnp.float32)
+        for slot in range(slots):
+            total = total + landed[slot, :, lo : lo + size].astype(jnp.float32)
         return total.astype(jnp.bfloat16)
 
     kind = k % 2
@@ -268,11 +312,12 @@
             relay(m).wait_send()
 
     for s in range(n):
-        block = c ^ s
+        block = block_of(s)
         for i in range(2 * len(peers) + 1):
             forward(s, block, k, k ^ 1, i).wait_send()
     for s in range(1, n):
-        part_copy(s).wait_send()
+        for i in (0, 1):
+            part_copy(s, i).wait_send()
     for i in (1, 2, 3):
         kv_copy(i).wait_send()
     seg_copy(0).wait_send()
@@ -302,7 +347,9 @@
             pltpu.VMEM((n, half // n, depth), jnp.bfloat16),
             pltpu.VMEM((depth, width), jnp.bfloat16),
             pltpu.VMEM((n - 1, half, width), jnp.bfloat16),
-            pltpu.VMEM((n - 1, half, width), jnp.bfloat16),
+            pltpu.VMEM((2 if n == 4 else n - 1, half, width), jnp.bfloat16),
+            pltpu.VMEM((2, half, width), jnp.bfloat16),
+            pltpu.VMEM((2, half, width), jnp.float32),
             pltpu.VMEM((half, width), jnp.float32),
             pltpu.VMEM((half, width - head), jnp.bfloat16),
             pltpu.VMEM((2, 4, half, head), jnp.bfloat16),
@@ -313,8 +360,9 @@
             dma((n,)),
             dma((n, n)),
             dma((n, n)),
-            dma((n - 1,)),
-            dma((n - 1,)),
+            dma((n - 1, 2)),
+            dma((n - 1, 2)),
+            dma((2, 2)),
             dma((8,)),
             dma((2, 4)),
             dma((3,)),

time: 84.7 us -> 80.8 us (0.954)
  the two profiles are of different devices: /device:TPU:19 before, /device:TPU:9 now
where the time goes in v3:
time: 80.8 us; the launch traced here: 80.6 us
  Pallas kernels  78.9 us (98%)
  local copies, waits for them, and re-layouts  1.67 us (2%)
    pallas_call x1, Pallas kernels, local(): pl.pallas_call(functools.partial(kernel, n, head), out_shape=jax.ShapeDty...  78.9 us
    unnamed x1, local copies, waits for them, and re-layouts  1.67 us

profile of v3, /device:TPU:9, one launch (start us, length us, event | category | flops | bytes accessed | tf_op | source)
XLA Modules:
  0.0 80.6 jit_solution(14659762744671908164)
XLA Ops:
  0.0 78.9 %shard_map.46 = bf16[256,512]{1,0:T(8,128)(2,1)} custom-call(bf16[256,2048]{1,0:T(8,128)(2,1)} %tok_hbm.1, bf16[2048,512]{1,0:T(8,128)(2,1)} %wq_hbm.1, bf16[2048,128]{1,0:T(8,128)(2,1)} %wkv_hbm.1, s32[1,256]{1,0:T(1,128)} %bitcast.1), custom_call_target="tpu_custom_call" | custom-call | tf_op jit(solution)/shard_map/pallas_call | solution.py:340
  78.9 1.7 %copy.6 = bf16[256,512]{1,0:T(8,128)(2,1)} copy(bf16[256,512]{1,0:T(8,128)(2,1)} %shard_map.46) | data formatting | bytes 524288

commit v4 on v3

--- a/solution.py
+++ b/solution.py
@@ -13,7 +13,7 @@
 
 def kernel(
     n, head, tok_hbm, wq_hbm, wkv_hbm, seg_ref, out_ref,
-    whole, staged, weights, part, landed, transit, far_own, own, query, window, segs,
+    whole, staged, weights, part, landed, transit, acc, query, window, segs,
     w_sem, a2a_send, stage_recv, relay_send, tok_recv, fwd_send, part_send, part_recv, transit_recv, kv_send, kv_recv, seg_send, seg_recv,
 ):
     c, r, k = lax.axis_index("ctx"), lax.axis_index("row"), lax.axis_index("col")
@@ -21,6 +21,9 @@
     rows = half // n
     width = weights.shape[1]
     paired = n == 4
+    parts = acc.shape[0] // n
+    span = tok_hbm.shape[1] // parts
+    own = acc.at[n * (parts - 1)]
     inner = (c == 1) | (c == 2)
 
     def block_of(s):
@@ -57,34 +60,34 @@
     ends = jnp.where(c == 0, 1, 0) + jnp.where(c == n - 1, 1, 0)
     pl.semaphore_wait(barrier, n * n - 1 + 6 - 2 * ends)
 
-    def piece(block, j):
-        return whole.at[block, pl.ds(pl.multiple_of(j * rows, rows), rows)]
+    def piece(block, j, f):
+        return whole.at[block, pl.ds(pl.multiple_of(j * rows, rows), rows), pl.ds(f * span, span)]
 
     def landing(ref, sem):
         return pltpu.make_async_copy(ref, ref, sem)
 
     own_plane = c == k
 
-    def token_rows(j):
-        return tok_hbm.at[pl.ds(pl.multiple_of(j * rows, rows), rows)]
-
-    def scatter(m, plane):
+    def token_rows(j, f):
+        return tok_hbm.at[pl.ds(pl.multiple_of(j * rows, rows), rows), pl.ds(f * span, span)]
+
+    def scatter(m, plane, f):
         j = k ^ m
         return pltpu.make_async_remote_copy(
-            src_ref=token_rows(j), dst_ref=piece(c, j), send_sem=a2a_send.at[m], recv_sem=tok_recv.at[c, j],
+            src_ref=token_rows(j, f), dst_ref=piece(c, j, f), send_sem=a2a_send.at[f, m], recv_sem=tok_recv.at[f, c, j],
             device_id=(plane, r, j), device_id_type=MESH,
         )
 
-    def stage(m):
+    def stage(m, f):
         j = k ^ m
         return pltpu.make_async_remote_copy(
-            src_ref=token_rows(j), dst_ref=staged.at[m], send_sem=a2a_send.at[m], recv_sem=stage_recv.at[m],
+            src_ref=token_rows(j, f), dst_ref=staged.at[f, m], send_sem=a2a_send.at[f, m], recv_sem=stage_recv.at[f, m],
             device_id=(c, r, j), device_id_type=MESH,
         )
 
-    def relay(m):
-        return pltpu.make_async_remote_copy(
-            src_ref=staged.at[m], dst_ref=piece(c, k), send_sem=relay_send.at[m], recv_sem=tok_recv.at[c, k],
+    def relay(m, f):
+        return pltpu.make_async_remote_copy(
+            src_ref=staged.at[f, m], dst_ref=piece(c, k, f), send_sem=relay_send.at[f, m], recv_sem=tok_recv.at[f, c, k],
             device_id=(k ^ m, r, k), device_id_type=MESH,
         )
 
@@ -92,17 +95,19 @@
 
     @pl.when(own_plane)
     def _():
-        for m in far:
-            scatter(m, c).start()
-        pltpu.make_async_copy(token_rows(k), piece(c, k), tok_recv.at[c, k]).start()
-        scatter(1, c).start()
+        for f in range(parts):
+            for m in far:
+                scatter(m, c, f).start()
+            pltpu.make_async_copy(token_rows(k, f), piece(c, k, f), tok_recv.at[f, c, k]).start()
+            scatter(1, c, f).start()
 
     @pl.when(c != k)
     def _():
-        for m in far:
-            stage(m).start()
-        for m in (1, 0):
-            scatter(m, k).start()
+        for f in range(parts):
+            for m in far:
+                stage(m, f).start()
+            for m in (1, 0):
+                scatter(m, k, f).start()
 
     segs[2 + r] = jnp.broadcast_to(seg_ref[...], segs.shape[1:])
 
@@ -121,34 +126,37 @@
         seg_copy(1).start()
         seg_copy(2).start()
 
-    for m in far:
-
-        @pl.when(c != k ^ m)
-        def _():
-            landing(staged.at[m], stage_recv.at[m]).wait()
-            relay(m).start()
-
-    def forward(s, block, j, to, index):
-        return pltpu.make_async_remote_copy(
-            src_ref=piece(block, j), dst_ref=piece(block, j),
-            send_sem=fwd_send.at[s, index], recv_sem=tok_recv.at[block, j],
+    def relays(f):
+        for m in far:
+
+            @pl.when(c != k ^ m)
+            def _():
+                landing(staged.at[f, m], stage_recv.at[f, m]).wait()
+                relay(m, f).start()
+
+    relays(0)
+
+    def forward(f, s, block, j, to, index):
+        return pltpu.make_async_remote_copy(
+            src_ref=piece(block, j, f), dst_ref=piece(block, j, f),
+            send_sem=fwd_send.at[f, s, index], recv_sem=tok_recv.at[f, block, j],
             device_id=(c, r, to), device_id_type=MESH,
         )
 
     peers = list(range(2, n, 2))
 
-    def step_a(s):
+    def step_a(f, s):
         block = block_of(s)
-        landing(piece(block, k), tok_recv.at[block, k]).wait()
+        landing(piece(block, k, f), tok_recv.at[f, block, k]).wait()
         for i, m in enumerate(peers):
-            forward(s, block, k, k ^ m, i).start()
-        forward(s, block, k, k ^ 1, len(peers)).start()
-
-    def step_b(s):
+            forward(f, s, block, k, k ^ m, i).start()
+        forward(f, s, block, k, k ^ 1, len(peers)).start()
+
+    def step_b(f, s):
         block = block_of(s)
         for i, m in enumerate(peers):
-            landing(piece(block, k ^ m), tok_recv.at[block, k ^ m]).wait()
-            forward(s, block, k ^ m, k ^ 1, len(peers) + 1 + i).start()
+            landing(piece(block, k ^ m, f), tok_recv.at[f, block, k ^ m]).wait()
+            forward(f, s, block, k ^ m, k ^ 1, len(peers) + 1 + i).start()
 
     chunk = half // 2
 
@@ -171,21 +179,28 @@
 
     spans = [(0, head)] + [(lo, min(256, width - lo)) for lo in range(head, width, 256)]
 
-    def step_c(s):
+    def step_c(f, s):
         block = block_of(s)
         for m in [0] + peers:
-            landing(piece(block, k ^ 1 ^ m), tok_recv.at[block, k ^ 1 ^ m]).wait()
-        if s == 0:
+            landing(piece(block, k ^ 1 ^ m, f), tok_recv.at[f, block, k ^ 1 ^ m]).wait()
+        if f == 0 and s == 0:
             for copy in w_copies:
                 copy.wait()
+        last = f == parts - 1
         for lo, size in spans:
-            product = jnp.dot(whole[block], weights[:, lo : lo + size], preferred_element_type=jnp.float32)
-            if s == 0:
-                own[:, lo : lo + size] = product
-            else:
+            product = jnp.dot(
+                whole[block, :, f * span : (f + 1) * span],
+                weights[f * span : (f + 1) * span, lo : lo + size],
+                preferred_element_type=jnp.float32,
+            )
+            if f:
+                product = product + acc[(f - 1) * n + s, :, lo : lo + size]
+            if not last or s == 0 or (paired and s >= 2):
+                acc[f * n + s, :, lo : lo + size] = product
+            if last and s:
                 part[s - 1, :, lo : lo + size] = product.astype(jnp.bfloat16)
-                if paired and s >= 2:
-                    far_own[s - 2, :, lo : lo + size] = product
+        if not last:
+            return
         if paired and s >= 2:
 
             @pl.when(jnp.logical_not(inner))
@@ -203,17 +218,21 @@
             for i in (0, 1):
                 lines = pl.ds(i * chunk, chunk)
                 landing(transit.at[s - 2, lines], transit_recv.at[s - 2, i]).wait()
-                total = far_own[s - 2, lines] + transit[s - 2, lines].astype(jnp.float32)
+                total = acc[n * (parts - 1) + s, lines] + transit[s - 2, lines].astype(jnp.float32)
                 part[s - 1, lines] = total.astype(jnp.bfloat16)
                 part_copy(s, i).start()
 
-    for t in range(n + 2):
-        if t < n:
-            step_a(t)
-        if 0 <= t - 1 < n:
-            step_b(t - 1)
-        if 0 <= t - 2 < n:
-            step_c(t - 2)
+    units = [(f, s) for f in range(parts) for s in range(n)]
+    for t in range(len(units) + 2):
+        if t == 1:
+            for f in range(1, parts):
+                relays(f)
+        if t < len(units):
+            step_a(*units[t])
+        if 0 <= t - 1 < len(units):
+            step_b(*units[t - 1])
+        if 0 <= t - 2 < len(units):
+            step_c(*units[t - 2])
 
     if paired:
         combine(2)
@@ -298,23 +317,24 @@
         numer = jnp.dot(weight.astype(jnp.bfloat16), values, preferred_element_type=jnp.float32)
         out_ref[:, h * head : (h + 1) * head] = (numer / total).astype(jnp.bfloat16)
 
-    for m in range(1, n):
-        stage(m).wait_send()
-
-    @pl.when(c != k)
-    def _():
-        stage(0).wait_send()
-
-    for m in far:
-
-        @pl.when(c != k ^ m)
+    for f in range(parts):
+        for m in range(1, n):
+            stage(m, f).wait_send()
+
+        @pl.when(c != k)
         def _():
-            relay(m).wait_send()
-
-    for s in range(n):
-        block = block_of(s)
-        for i in range(2 * len(peers) + 1):
-            forward(s, block, k, k ^ 1, i).wait_send()
+            stage(0, f).wait_send()
+
+        for m in far:
+
+            @pl.when(c != k ^ m)
+            def _():
+                relay(m, f).wait_send()
+
+        for s in range(n):
+            block = block_of(s)
+            for i in range(2 * len(peers) + 1):
+                forward(f, s, block, k, k ^ 1, i).wait_send()
     for s in range(1, n):
         for i in (0, 1):
             part_copy(s, i).wait_send()
@@ -334,6 +354,7 @@
     half, depth = tokens.shape
     head = key_value_weight.shape[1]
     width = head + w_query.shape[1]
+    parts = 2 if n == 4 else 1
     hbm = pl.BlockSpec(memory_space=pl.ANY)
     vmem = pl.BlockSpec(memory_space=pltpu.VMEM)
     dma = pltpu.SemaphoreType.DMA
@@ -344,22 +365,21 @@
         out_specs=vmem,
         scratch_shapes=[
             pltpu.VMEM((n, half, depth), jnp.bfloat16),
-            pltpu.VMEM((n, half // n, depth), jnp.bfloat16),
+            pltpu.VMEM((parts, n, half // n, depth // parts), jnp.bfloat16),
             pltpu.VMEM((depth, width), jnp.bfloat16),
             pltpu.VMEM((n - 1, half, width), jnp.bfloat16),
             pltpu.VMEM((2 if n == 4 else n - 1, half, width), jnp.bfloat16),
             pltpu.VMEM((2, half, width), jnp.bfloat16),
-            pltpu.VMEM((2, half, width), jnp.float32),
-            pltpu.VMEM((half, width), jnp.float32),
+            pltpu.VMEM((parts * n, half, width), jnp.float32),
             pltpu.VMEM((half, width - head), jnp.bfloat16),
             pltpu.VMEM((2, 4, half, head), jnp.bfloat16),
             pltpu.VMEM((4, 8, half), jnp.int32),
             dma((2,)),
-            dma((n,)),
-            dma((n,)),
-            dma((n,)),
-            dma((n, n)),
-            dma((n, n)),
+            dma((parts, n)),
+            dma((parts, n)),
+            dma((parts, n)),
+            dma((parts, n, n)),
+            dma((parts, n, n)),
             dma((n - 1, 2)),
             dma((n - 1, 2)),
             dma((2, 2)),

time: 80.8 us -> 82.3 us (1.019); the launches traced: 80.6 us -> 81.2 us
  no operation moved by 1% of the time
where the time goes in v4:
time: 82.3 us; the launch traced here: 81.2 us
  Pallas kernels  79.5 us (97%)
  local copies, waits for them, and re-layouts  1.67 us (2%)
    pallas_call x1, Pallas kernels, local(): pl.pallas_call(functools.partial(kernel, n, head), out_shape=jax.ShapeDty...  79.5 us
    unnamed x1, local copies, waits for them, and re-layouts  1.67 us

profile of v4, /device:TPU:9, one launch (start us, length us, event | category | flops | bytes accessed | tf_op | source)
XLA Modules:
  0.0 81.2 jit_solution(6751371865916906657)
XLA Ops:
  0.0 79.5 %shard_map.46 = bf16[256,512]{1,0:T(8,128)(2,1)} custom-call(bf16[256,2048]{1,0:T(8,128)(2,1)} %tok_hbm.1, bf16[2048,512]{1,0:T(8,128)(2,1)} %wq_hbm.1, bf16[2048,128]{1,0:T(8,128)(2,1)} %wkv_hbm.1, s32[1,256]{1,0:T(1,128)} %bitcast.1), custom_call_target="tpu_custom_call" | custom-call | tf_op jit(solution)/shard_map/pallas_call | solution.py:361
  79.5 1.7 %copy.6 = bf16[256,512]{1,0:T(8,128)(2,1)} copy(bf16[256,512]{1,0:T(8,128)(2,1)} %shard_map.46) | data formatting | bytes 524288

commit v5 on v3

--- a/solution.py
+++ b/solution.py
@@ -150,7 +150,7 @@
             landing(piece(block, k ^ m), tok_recv.at[block, k ^ m]).wait()
             forward(s, block, k ^ m, k ^ 1, len(peers) + 1 + i).start()
 
-    chunk = half // 2
+    chunk = half // 4
 
     def part_copy(s, i):
         lines = pl.ds(i * chunk, chunk)
@@ -190,17 +190,17 @@
 
             @pl.when(jnp.logical_not(inner))
             def _():
-                for i in (0, 1):
+                for i in range(4):
                     hand_over(s, i).start()
 
         elif s:
-            for i in (0, 1):
+            for i in range(4):
                 part_copy(s, i).start()
 
     def combine(s):
         @pl.when(inner)
         def _():
-            for i in (0, 1):
+            for i in range(4):
                 lines = pl.ds(i * chunk, chunk)
                 landing(transit.at[s - 2, lines], transit_recv.at[s - 2, i]).wait()
                 total = far_own[s - 2, lines] + transit[s - 2, lines].astype(jnp.float32)
@@ -221,7 +221,7 @@
 
     slots = landed.shape[0]
     for slot in range(slots):
-        for i in (0, 1):
+        for i in range(4):
             landing(landed.at[slot, pl.ds(i * chunk, chunk)], part_recv.at[slot, i]).wait()
 
     def summed(lo, size):
@@ -316,7 +316,7 @@
         for i in range(2 * len(peers) + 1):
             forward(s, block, k, k ^ 1, i).wait_send()
     for s in range(1, n):
-        for i in (0, 1):
+        for i in range(4):
             part_copy(s, i).wait_send()
     for i in (1, 2, 3):
         kv_copy(i).wait_send()
@@ -360,9 +360,9 @@
             dma((n,)),
             dma((n, n)),
             dma((n, n)),
-            dma((n - 1, 2)),
-            dma((n - 1, 2)),
-            dma((2, 2)),
+            dma((n - 1, 4)),
+            dma((n - 1, 4)),
+            dma((2, 4)),
             dma((8,)),
             dma((2, 4)),
             dma((3,)),

time: 80.8 us -> 79.1 us (0.979)
  Pallas kernels: 78.9 us -> 77.3 us
    pallas_call x1, Pallas kernels: 78.9 us -> 77.3 us  [local(): pl.pallas_call(functools.partial(kernel, n, head), out_shape=jax.ShapeDty...]
where the time goes in v5:
time: 79.1 us; the launch traced here: 79 us
  Pallas kernels  77.3 us (98%)
  local copies, waits for them, and re-layouts  1.67 us (2%)
    pallas_call x1, Pallas kernels, local(): pl.pallas_call(functools.partial(kernel, n, head), out_shape=jax.ShapeDty...  77.3 us
    unnamed x1, local copies, waits for them, and re-layouts  1.67 us

profile of v5, /device:TPU:9, one launch (start us, length us, event | category | flops | bytes accessed | tf_op | source)
XLA Modules:
  0.0 79.0 jit_solution(11393539603269577785)
XLA Ops:
  0.0 77.3 %shard_map.46 = bf16[256,512]{1,0:T(8,128)(2,1)} custom-call(bf16[256,2048]{1,0:T(8,128)(2,1)} %tok_hbm.1, bf16[2048,512]{1,0:T(8,128)(2,1)} %wq_hbm.1, bf16[2048,128]{1,0:T(8,128)(2,1)} %wkv_hbm.1, s32[1,256]{1,0:T(1,128)} %bitcast.1), custom_call_target="tpu_custom_call" | custom-call | tf_op jit(solution)/shard_map/pallas_call | solution.py:340
  77.3 1.7 %copy.6 = bf16[256,512]{1,0:T(8,128)(2,1)} copy(bf16[256,512]{1,0:T(8,128)(2,1)} %shard_map.46) | data formatting | bytes 524288
